TPU v7x, 32 devices: a whole 2x2x4 slice. The times are simulated.
32 devices in a mesh: shift: 4 (over y, x), rows: 8 (over z, core).
Axes of the slice: x: 2, y: 2, z: 4, core: 2. Of those that a mesh axis runs over, the one named last changes fastest.
Arguments:
- zc_in: bfloat16 [4, 512, 16384], P('shift', 'rows'), may hold values from -6 to 6
- zo_in: bfloat16 [4, 384, 16384], P('shift', 'rows'), may hold values from -6 to 6
- count_c: int32 [4], replicated, may hold values from 256 to 512, as said below
- count_o: int32 [4], replicated, may hold values from 192 to 384, as said below
- mass: bfloat16 [128, 4, 128, 128], P(('shift', 'rows')), may hold values from -0.25 to 0.25
- adjacency: int32 [128, 4], P(('shift', 'rows')), may hold values from 0 to 127, as said below
- ghost_len: int32 [128, 4], P(('shift', 'rows')), may hold values from 1 to 128, as said below
- omega: float32 [2048, 128], replicated, may hold values from -6 to 6
Outputs:
- proj_c: float32 [128, 16384], P(None, ('shift', 'rows'))
- proj_o: float32 [128, 16384], P(None, ('shift', 'rows'))
Inputs may be any that keep to these rules, and one draw needn't show every extreme that they name: `count_c`: each entry is 256 or more, and one group holds 512 exactly. `count_o`: each entry is 192 or more, and one group holds 384 exactly. adjacency[i, 0] = i, and every entry lies within 2 blocks of i. ghost_len[i, 0] = 128.
All inputs are finite; a program needn't handle non-finite values.
Results may differ from a plain program's by a relative error of at most 0.0047.
Values may be sent and summed in bfloat16 or wider, within the bound.
A program may use at most 128 MiB of HBM per device.

v0:
```python
import jax
import jax.numpy as jnp
from jax import lax
from jax.sharding import PartitionSpec as P

REACH = 2


def padded(shard, sides, width):
    for axis, dim in sides:
        size, length = (lax.axis_size(axis), shard.shape[dim])
        up = [(i, (i + 1) % size) for i in range(size - 1)]
        down = [(j, i) for i, j in up]
        last = lax.slice_in_dim(shard, length - width, length, axis=dim)
        initial = lax.slice_in_dim(shard, 0, width, axis=dim)
        before = lax.ppermute(last, axis, up)
        after = lax.ppermute(initial, axis, down)
        shard = jnp.concatenate([before, shard, after], axis=dim)
    return shard


def prepare(factor, counts, group, member):
    width = factor.shape[1]
    slots = member * width + jnp.arange(width, dtype=jnp.int32)
    keep = slots < counts[group]
    return jnp.where(keep[:, None], factor[0], jnp.zeros_like(factor[0]))


def orth_local(matrix):
    square = jnp.dot(matrix.T, matrix, precision=lax.Precision.HIGHEST)
    lower = jnp.linalg.cholesky(square)
    return jax.scipy.linalg.solve_triangular(lower, matrix.T, lower=True).T


def per_device(zc_in, zo_in, count_c, count_o, mass, adjacency, ghost_len, omega):
    group = lax.axis_index("shift")
    member = lax.axis_index("rows")
    members = lax.axis_size("rows")
    part_c = prepare(zc_in, count_c, group, member)
    part_o = prepare(zo_in, count_o, group, member)
    zc, zo = (
        lax.all_to_all(part_c, ("shift", "rows"), split_axis=1, concat_axis=0, tiled=True),
        lax.all_to_all(part_o, ("shift", "rows"), split_axis=1, concat_axis=0, tiled=True),
    )
    width_c = zc.shape[0]
    rows_here = zc.shape[1]
    block_size = mass.shape[2]
    count_blocks = rows_here // block_size
    extended = padded(zc, ((("shift", "rows"), 1),), REACH * block_size)
    first_block = (group * members + member) * count_blocks
    local_index = (adjacency - first_block + REACH).reshape(-1)
    blocks = extended.reshape(width_c, count_blocks + 2 * REACH, block_size)
    pieces = jnp.take(blocks, local_index, axis=1).reshape(
        width_c, count_blocks, adjacency.shape[1], block_size
    )
    inner = jnp.arange(block_size, dtype=jnp.int32)
    keep = inner[None, None, None, :] < ghost_len[:, :, None, None]
    masked = jnp.where(keep, mass, jnp.zeros_like(mass))
    mixed = jnp.einsum("cikp,ikqp->ciq", pieces, masked, preferred_element_type=jnp.float32)
    mixed = mixed.astype(jnp.bfloat16).reshape(width_c, rows_here)
    high = lax.Precision.HIGHEST
    partial_gram = lax.dot_general(
        zo, mixed, (((1,), (1,)), ((), ())), preferred_element_type=jnp.float32
    )
    gram = lax.psum(partial_gram, ("shift", "rows"))
    first = orth_local(jnp.dot(gram, omega, precision=high))
    right = orth_local(jnp.dot(gram.T, first, precision=high))
    left = orth_local(jnp.dot(gram, right, precision=high))
    proj_c = jnp.dot(right.astype(jnp.bfloat16).T, zc, preferred_element_type=jnp.float32)
    proj_o = jnp.dot(left.astype(jnp.bfloat16).T, zo, preferred_element_type=jnp.float32)
    return (proj_c, proj_o)


def solution(mesh):
    placed = (
        P("shift", "rows", None),
        P("shift", "rows", None),
        P(),
        P(),
        P(("shift", "rows"), None, None, None),
        P(("shift", "rows"), None),
        P(("shift", "rows"), None),
        P(),
    )
    return jax.shard_map(
        per_device,
        mesh=mesh,
        in_specs=placed,
        out_specs=(P(None, ("shift", "rows")), P(None, ("shift", "rows"))),
        check_vma=False,
    )
```

profile of v0, /device:TPU:0, one launch (start us, length us, event | category | flops | bytes accessed | tf_op | source)
XLA Modules:
  0.0 544.4 jit_solution(15689129905431404123)
XLA Ops:
  7.2 0.0 copy-start
  7.2 0.0 copy-start.5
  7.2 2.4 copy.32
  9.6 0.0 copy-done.5
  9.7 0.6 dynamic_slice.7
  10.2 0.7 add_compare_fusion
  10.9 0.4 bitcast_select_fusion
  11.3 0.0 copy-start.6
  11.3 2.5 copy.24
  13.8 7.3 %all-to-all-start.1 = ((bf16[64,32,512]{2,0,1:T(8,128)(2,1)}), bf16[64,32,512]{2,0,1:T(8,128)(2,1)S(1)}, u32[]{:S(2)}, u32[]{:S(2)}) async-start(bf16[64,32,512]{2,0,1:T(8,128)(2,1)} %copy.24), calls=%async_computation.1 | async-start | bytes 4194304 | tf_op jit(solution)/shard_map/all_to_all | solution.py:42
  21.1 0.6 dynamic_slice.6
  21.7 2.0 copy.31
  23.7 0.7 add_compare_fusion.1
  24.3 0.3 bitcast_select_fusion.1
  24.6 2.1 copy.23
  26.7 44.5 %all-to-all-done.1 = bf16[64,32,512]{2,0,1:T(8,128)(2,1)S(1)} async-done(((bf16[64,32,512]{2,0,1:T(8,128)(2,1)}), bf16[64,32,512]{2,0,1:T(8,128)(2,1)S(1)}, u32[]{:S(2)}, u32[]{:S(2)}) %all-to-all-start.1) | async-done | bytes 2097184 | tf_op jit(solution)/shard_map/all_to_all | solution.py:42
  71.2 3.4 all-to-all-start
  74.6 0.0 all-reduce.2.cloned.1.call-start
  74.7 1.5 fusion.29
  76.2 3.0 collective-permute-start
  79.1 1.5 collective-permute-start.1
  80.6 0.1 reshape.99
  80.8 0.1 iota_compare_fusion.2
  80.8 0.0 collective-permute-done
  80.8 3.4 collective-permute-done.1
  84.2 3.4 pad_maximum_fusion
  87.6 6.5 %copy.25 = bf16[2048,1024]{0,1:T(8,128)(2,1)} copy(bf16[2048,1024]{1,0:T(8,128)(2,1)} %pad_maximum_fusion) | data formatting | bytes 8388608 | tf_op jit(solution)/shard_map/concatenate | solution.py:18
  94.1 6.5 %copy.26 = bf16[2048,8,128]{2,0,1:T(8,128)(2,1)} copy(bf16[2048,8,128]{0,2,1:T(8,128)(2,1)} %bitcast.82) | data formatting | bytes 8388608 | tf_op jit(solution)/shard_map/reshape | solution.py:52
  100.6 6.9 %gather_fusion = bf16[16,2048,128]{2,1,0:T(8,128)(2,1)} fusion(bf16[2048,8,128]{2,0,1:T(8,128)(2,1)} %copy.26, s32[1024]{0:T(1024)S(1)} %pad_clamp_fusion), kind=kCustom, calls=%fused_computation | custom fusion | bytes 16777280 | tf_op jit(solution)/shard_map/jit(_take)/gather | solution.py:53
  107.5 7.8 %bitcast_convert_fusion = bf16[4,128,2048]{2,1,0:T(8,128)(2,1)} fusion(bf16[2048,4,4,128]{3,0,2,1:T(8,128)(2,1)} %bitcast.83, pred[4,4]{1,0:T(4,128)(4,1)S(1)} %compare_and_fusion, bf16[4,4,128,128]{3,2,1,0:T(8,128)(2,1)} %param.15, pred[4,4,128]{2,1,0:T(4,128)(4,1)S(1)} %iota_compare_fusion.2), kind=kOutput, calls=%fused_computation.5 | convolution fusion | flops 1079246848 | bytes 11012112 | tf_op jit(solution)/shard_map/cikp,ikqp->ciq/dot_general | solution.py:59
  115.3 0.0 all-to-all-done
  115.3 10.0 %fusion.30 = f32[1536,2048]{1,0:T(8,128)} fusion(bf16[1536,512]{1,0:T(8,128)(2,1)} %bitcast.2, bf16[2048,512]{0,1:T(8,128)(2,1)} %bitcast.86), kind=kOutput, calls=%fused_computation.55 | convolution fusion | flops 3221225472 | bytes 16252928 | tf_op jit(solution)/shard_map/dot_general | solution.py:62
  125.3 0.0 all-reduce.2.cloned.1.call-update
  125.4 278.8 %all-reduce.2.cloned.1.call-done = f32[1536,2048]{1,0:T(8,128)} async-done(((f32[1536,2048]{1,0:T(8,128)}), f32[1536,2048]{1,0:T(8,128)}) %all-reduce.2.cloned.1.call-update) | async-done | bytes 12582928 | tf_op jit(solution)/shard_map/psum | solution.py:65
  404.2 0.0 copy-done
  404.2 12.7 %fusion.31 = f32[1536,128]{1,0:T(8,128)S(1)} fusion(f32[1536,2048]{1,0:T(8,128)} %all-reduce.2.cloned.1.call-done, f32[2048,128]{1,0:T(8,128)S(1)} %copy-done), kind=kOutput, calls=%fused_computation.56 | convolution fusion | flops 4831838208 | bytes 14417920 | tf_op jit(solution)/shard_map/dot_general | solution.py:66
  416.9 0.9 copy-done.2
  417.8 1.5 fusion.32
  419.3 0.1 copy.27
  419.4 11.7 %cholesky.59 = f32[128,128]{1,0:T(8,128)S(1)} custom-call(f32[128,128]{1,0:T(8,128)S(1)} %fusion.23), custom_call_target="Cholesky" | custom-call | tf_op jit(solution)/shard_map/jit(cholesky)/cholesky | solution.py:31
  431.1 0.6 compare_reduce_fusion.2
  431.8 0.7 fusion.14
  432.4 9.8 %custom-call.11 = f32[1,128,128]{1,2,0:T(8,128)S(1)} custom-call(f32[1,128,128]{2,1,0:T(8,128)S(1)} %fusion.14), custom_call_target="InvertDiagBlocksLowerTriangular" | custom-call | tf_op jit(solution)/shard_map/jit(_solve_triangular)/triangular_solve | solution.py:32
  442.3 2.0 fusion.7
  444.2 23.2 %fusion.33 = f32[2048,128]{1,0:T(8,128)S(1)} fusion(f32[1536,2048]{1,0:T(8,128)} %all-reduce.2.cloned.1.call-done, f32[128,1536]{1,0:T(8,128)S(1)} %fusion.7), kind=kOutput, calls=%fused_computation.58 | convolution fusion | flops 4831838208 | bytes 14417920 | tf_op jit(solution)/shard_map/dot_general | solution.py:67
  467.5 0.0 copy-start.1
  467.5 1.0 copy-done.1
  468.5 1.9 fusion.34
  470.4 0.1 copy.28
  470.5 11.7 %cholesky.70 = f32[128,128]{1,0:T(8,128)S(1)} custom-call(f32[128,128]{1,0:T(8,128)S(1)} %fusion.21), custom_call_target="Cholesky" | custom-call | tf_op jit(solution)/shard_map/jit(cholesky)/cholesky | solution.py:31
  482.3 0.6 compare_reduce_fusion.1
  482.9 0.7 fusion.15
  483.6 9.8 %custom-call.9 = f32[1,128,128]{1,2,0:T(8,128)S(1)} custom-call(f32[1,128,128]{2,1,0:T(8,128)S(1)} %fusion.15), custom_call_target="InvertDiagBlocksLowerTriangular" | custom-call | tf_op jit(solution)/shard_map/jit(_solve_triangular)/triangular_solve | solution.py:32
  493.4 2.3 fusion.19
  495.7 1.2 fusion.9
  496.9 12.7 %fusion.35 = f32[1536,128]{1,0:T(8,128)S(1)} fusion(f32[1536,2048]{1,0:T(8,128)} %all-reduce.2.cloned.1.call-done, f32[128,2048]{1,0:T(8,128)S(1)} %fusion.19), kind=kOutput, calls=%fused_computation.60 | convolution fusion | flops 4831838208 | bytes 14417920 | tf_op jit(solution)/shard_map/dot_general | solution.py:68
  509.5 1.4 fusion.36
  511.0 0.1 copy.29
  511.1 11.7 %cholesky.81 = f32[128,128]{1,0:T(8,128)S(1)} custom-call(f32[128,128]{1,0:T(8,128)S(1)} %fusion.18), custom_call_target="Cholesky" | custom-call | tf_op jit(solution)/shard_map/jit(cholesky)/cholesky | solution.py:31
  522.8 0.6 compare_reduce_fusion
  523.5 0.7 fusion.16
  524.1 9.8 %custom-call.12 = f32[1,128,128]{1,2,0:T(8,128)S(1)} custom-call(f32[1,128,128]{2,1,0:T(8,128)S(1)} %fusion.16), custom_call_target="InvertDiagBlocksLowerTriangular" | custom-call | tf_op jit(solution)/shard_map/jit(_solve_triangular)/triangular_solve | solution.py:32
  533.9 0.9 convolution_convert_fusion
  534.8 2.5 fusion.37
  (16 shorter events, 0.2 us)
Async XLA Ops:
  7.2 397.0 %copy-start = (f32[2048,128]{1,0:T(8,128)S(1)}, f32[2048,128]{1,0:T(8,128)}, u32[]{:S(2)}) copy-start(f32[2048,128]{1,0:T(8,128)} %param.18) | copy-start | bytes 3145732
  7.2 2.5 copy-start.5
  11.3 9.8 %copy-start.6 = (s32[4]{0:T(128)S(1)}, s32[4]{0:T(128)}, u32[]{:S(2)}) copy-start(s32[4]{0:T(128)} %param.14) | copy-start | bytes 52
  13.8 57.4 %all-to-all-start.1 = ((bf16[64,32,512]{2,0,1:T(8,128)(2,1)}), bf16[64,32,512]{2,0,1:T(8,128)(2,1)S(1)}, u32[]{:S(2)}, u32[]{:S(2)}) async-start(bf16[64,32,512]{2,0,1:T(8,128)(2,1)} %copy.24), calls=%async_computation.1 | async-start | bytes 4194304 | tf_op jit(solution)/shard_map/all_to_all | solution.py:42
  26.7 53.9 %copy-start.3 = (s32[4,4]{1,0:T(4,128)S(1)}, s32[4,4]{1,0:T(4,128)}, u32[]{:S(2)}) copy-start(s32[4,4]{1,0:T(4,128)} %param.16) | copy-start | bytes 196
  26.7 54.0 %copy-start.4 = (s32[4,4]{1,0:T(4,128)S(1)}, s32[4,4]{1,0:T(4,128)}, u32[]{:S(2)}) copy-start(s32[4,4]{1,0:T(4,128)} %param.17) | copy-start | bytes 196
  71.2 44.1 %all-to-all-start = ((bf16[48,32,512]{2,0,1:T(8,128)(2,1)}), bf16[48,32,512]{2,0,1:T(8,128)(2,1)}, u32[]{:S(2)}, u32[]{:S(2)}) async-start(bf16[48,32,512]{2,0,1:T(8,128)(2,1)} %copy.23), calls=%async_computation | async-start | bytes 3145728 | tf_op jit(solution)/shard_map/all_to_all | solution.py:43
  74.6 329.6 %all-reduce.2.cloned.1.call-start = ((), (), s32[]{:S(2)}) async-start(), calls=%async_computation.2 | async-start | bytes 25165824 | tf_op jit(solution)/shard_map/psum | solution.py:65
  76.2 4.7 collective-permute-start
  79.1 5.1 collective-permute-start.1
  416.9 0.9 copy-start.2
  467.5 1.1 copy-start.1
Sparse Core Ops, SparseCore 0:
  125.5 278.6 all-reduce.1
where the time goes:
time: 549 us; the launch traced here: 544 us
  waiting for transfers between devices  327 us (60%)
  matrix products  80 us (15%)
  other arithmetic  74.1 us (13%)
  local copies, waits for them, and re-layouts  33.9 us (6%)
  starting transfers between devices  15.2 us (3%)
  between operations  14.6 us (3%)
    psum x1, waiting for transfers between devices, per_device(): gram = lax.psum(partial_gram, ('shift', 'rows'))  279 us
    all_to_all x1, waiting for transfers between devices, per_device(): lax.all_to_all(part_c, ('shift', 'rows'), split_axis=1, concat_axis=0, ti...  44.5 us
    another operation x9, other arithmetic, orth_local(): lower = jnp.linalg.cholesky(square)  37.2 us
    another operation x6, other arithmetic, orth_local(): return jax.scipy.linalg.solve_triangular(lower, matrix.T, lower=True).T  31.4 us
    dot_general x1, matrix products, per_device(): right = orth_local(jnp.dot(gram.T, first, precision=high))  23.2 us
    dot_general x1, matrix products, per_device(): first = orth_local(jnp.dot(gram, omega, precision=high))  12.7 us
    dot_general x1, matrix products, per_device(): left = orth_local(jnp.dot(gram, right, precision=high))  12.7 us
  transfers between devices with their start and end apart: 5, of which 3 were waited for; matrix products, arithmetic and copies ran while one was open for 7% of the time, Pallas kernels for 0%

commit v1 on v0

v1 whole, which is shorter than its diff:
```python
import jax
import jax.numpy as jnp
from jax import lax
from jax.sharding import PartitionSpec as P

REACH = 2
AXES = ("shift", "rows")
F32 = jnp.float32
BF16 = jnp.bfloat16


def split(matrix):
    high = lax.reduce_precision(matrix, 8, 7)
    return jnp.concatenate([high.astype(BF16), (matrix - high).astype(BF16)], axis=-1)


def joined(matrix):
    half = matrix.shape[-1] // 2
    return matrix[..., :half] + matrix[..., half:]


def dot(left, right, contract_left, contract_right):
    return lax.dot_general(
        left, right, (((contract_left,), (contract_right,)), ((), ())), preferred_element_type=F32
    )


def live(counts, slots):
    inner = jnp.arange(slots, dtype=jnp.int32)
    return (inner[None, :] < counts[:, None]).reshape(-1, 1)


def orth_local(matrix):
    square = jnp.dot(matrix.T, matrix, precision=lax.Precision.HIGHEST)
    lower = jnp.linalg.cholesky(square)
    return jax.scipy.linalg.solve_triangular(lower, matrix.T, lower=True).T


def per_device(zc_in, zo_in, count_c, count_o, mass, adjacency, ghost_len, omega):
    index = lax.axis_index(AXES)
    devices = lax.axis_size(AXES)
    zc = lax.all_to_all(zc_in[0], AXES, split_axis=1, concat_axis=0, tiled=True)
    zo = lax.all_to_all(zo_in[0], AXES, split_axis=1, concat_axis=0, tiled=True)
    groups = count_c.shape[0]
    live_c = live(count_c, zc.shape[0] // groups)
    live_o = live(count_o, zo.shape[0] // groups)
    size = mass.shape[2]
    count, near = adjacency.shape
    local = adjacency - index * count + REACH
    inner = jnp.arange(size, dtype=jnp.int32)
    masked = jnp.where(inner < ghost_len[:, :, None, None], mass, jnp.zeros_like(mass))
    places = jnp.arange(count + 2 * REACH, dtype=jnp.int32)
    hit = (local[:, :, None] == places)[:, :, None, :, None]
    dense = jnp.where(hit, masked[:, :, :, None, :].astype(F32), 0.0).sum(axis=1)
    dense = dense.reshape(count * size, -1)
    banded = lax.reduce_precision(dense, 8, 7)
    banded_rest = (dense - banded).astype(BF16)
    banded = banded.astype(BF16)
    up = [(i, i + 1) for i in range(devices - 1)]
    down = [(j, i) for i, j in up]
    edge = REACH * size
    width = omega.shape[1]

    def forward(right):
        rows = joined(dot(zc, split(right), 0, 0))
        before = lax.ppermute(rows[-edge:], AXES, up)
        after = lax.ppermute(rows[:edge], AXES, down)
        wide = split(jnp.concatenate([before, rows, after], axis=0))
        mixed = joined(dot(banded, wide, 1, 0) + dot(banded_rest, wide, 1, 0))
        part = joined(dot(zo, split(mixed), 1, 0))
        return jnp.where(live_o, lax.psum(part, AXES), 0.0)

    def backward(left):
        rows = dot(zo, split(left), 0, 0)
        rows = split(joined(rows))
        wide = joined(dot(banded, rows, 0, 0) + dot(banded_rest, rows, 0, 0))
        above = lax.ppermute(wide[-edge:], AXES, up)
        below = lax.ppermute(wide[:edge], AXES, down)
        rows = wide[edge:-edge]
        rows = rows + jnp.pad(above, ((0, rows.shape[0] - edge), (0, 0)))
        rows = rows + jnp.pad(below, ((rows.shape[0] - edge, 0), (0, 0)))
        part = joined(dot(zc, split(rows), 1, 0))
        return jnp.where(live_c, lax.psum(part, AXES), 0.0)

    first = orth_local(forward(jnp.where(live_c, omega, 0.0)))
    right = orth_local(backward(first))
    proj_c = dot(right.astype(BF16), zc, 0, 0)
    left = orth_local(forward(right))
    proj_o = dot(left.astype(BF16), zo, 0, 0)
    return (proj_c, proj_o)


def solution(mesh):
    placed = (
        P("shift", "rows", None),
        P("shift", "rows", None),
        P(),
        P(),
        P(AXES, None, None, None),
        P(AXES, None),
        P(AXES, None),
        P(),
    )
    return jax.shard_map(
        per_device,
        mesh=mesh,
        in_specs=placed,
        out_specs=(P(None, AXES), P(None, AXES)),
        check_vma=False,
    )
```

time: 549 us -> 638 us (1.16)
  waiting for transfers between devices: 327 us -> 482 us
  matrix products: 80 us -> 27.9 us
  local copies, waits for them, and re-layouts: 33.9 us -> 11.7 us
    psum x1 -> x3, waiting for transfers between devices: 279 us -> 400 us  [the longest x2 263 us: forward(): return jnp.where(live_o, lax.psum(part, AXES), 0.0)]
    dot_general x7 -> x14, matrix products: 70.1 us -> 14.9 us  [dot(): lax.dot_general(left, right, (((contract_left,), (contract_right,)), ((),...]
    all_to_all x2, waiting for transfers between devices: 44.5 us -> 73.4 us  [the longest x1 46 us: per_device(): zc = lax.all_to_all(zc_in[0], AXES, split_axis=1, concat_axis=0, tiled=True)]
    gather x1 -> x0, local copies, waits for them, and re-layouts: 6.91 us -> none  [per_device(): jnp.take(blocks, local_index, axis=1)]
    reshape x2 -> x0, local copies, waits for them, and re-layouts: 6.54 us -> none  [the longest x1 6.46 us: per_device(): blocks = extended.reshape(width_c, count_blocks + 2 * REACH, block_size)]
    concatenate x1 -> x0, local copies, waits for them, and re-layouts: 6.52 us -> none  [padded(): shard = jnp.concatenate([before, shard, after], axis=dim)]
  transfers between devices with their start and end apart: 5 -> 11, of which waited for: 3 -> 8; matrix products, arithmetic and copies ran while one was open for 7% -> 2% of each run, Pallas kernels for 0% -> 0%
where the time goes in v1:
time: 638 us; the launch traced here: 631 us
  waiting for transfers between devices  482 us (76%)
  other arithmetic  74.7 us (12%)
  matrix products  27.9 us (4%)
  starting transfers between devices  20.1 us (3%)
  between operations  14.7 us (2%)
  local copies, waits for them, and re-layouts  11.7 us (2%)
    psum x2, waiting for transfers between devices, forward(): return jnp.where(live_o, lax.psum(part, AXES), 0.0)  263 us
    psum x1, waiting for transfers between devices, backward(): return jnp.where(live_c, lax.psum(part, AXES), 0.0)  136 us
    all_to_all x1, waiting for transfers between devices, per_device(): zc = lax.all_to_all(zc_in[0], AXES, split_axis=1, concat_axis=0, tiled=True)  46 us
    another operation x9, other arithmetic, orth_local(): lower = jnp.linalg.cholesky(square)  37.2 us
    another operation x6, other arithmetic, orth_local(): return jax.scipy.linalg.solve_triangular(lower, matrix.T, lower=True).T  31.4 us
    all_to_all x1, waiting for transfers between devices, per_device(): zo = lax.all_to_all(zo_in[0], AXES, split_axis=1, concat_axis=0, tiled=True)  27.3 us
    dot_general x14, matrix products, dot(): lax.dot_general(left, right, (((contract_left,), (contract_right,)), ((),...  14.9 us
  transfers between devices with their start and end apart: 11, of which 8 were waited for; matrix products, arithmetic and copies ran while one was open for 2% of the time, Pallas kernels for 0%

profile of v1, /device:TPU:0, one launch (start us, length us, event | category | flops | bytes accessed | tf_op | source)
XLA Modules:
  0.0 631.5 jit_solution(16880807980116318967)
XLA Ops:
  7.2 2.4 copy.38
  9.5 2.5 copy.31
  12.0 7.3 %all-to-all-start = ((bf16[64,32,512]{2,0,1:T(8,128)(2,1)}), bf16[64,32,512]{2,0,1:T(8,128)(2,1)S(1)}, u32[]{:S(2)}, u32[]{:S(2)}) async-start(bf16[64,32,512]{2,0,1:T(8,128)(2,1)} %copy.31), calls=%async_computation | async-start | bytes 4194304 | tf_op jit(solution)/shard_map/all_to_all | solution.py:42
  19.3 2.0 copy.39
  21.3 2.0 copy.32
  23.4 46.0 %all-to-all-done = bf16[64,32,512]{2,0,1:T(8,128)(2,1)S(1)} async-done(((bf16[64,32,512]{2,0,1:T(8,128)(2,1)}), bf16[64,32,512]{2,0,1:T(8,128)(2,1)S(1)}, u32[]{:S(2)}, u32[]{:S(2)}) %all-to-all-start) | async-done | bytes 2097184 | tf_op jit(solution)/shard_map/all_to_all | solution.py:42
  69.4 3.5 all-to-all-start.1
  73.1 1.6 copy.30
  74.7 1.1 select_convert_fusion
  75.8 0.2 reduce-precision_convert_fusion.2
  76.0 0.7 convolution_bitcast_fusion.6
  76.8 2.0 collective-permute-start
  78.8 1.3 collective-permute-start.1
  80.1 0.9 select_reduce_fusion
  81.0 2.2 collective-permute-done.1
  83.3 0.5 fusion.42
  83.8 0.5 convolution_add_fusion.2
  84.4 27.3 %all-to-all-done.1 = bf16[48,32,512]{2,0,1:T(8,128)(2,1)} async-done(((bf16[48,32,512]{2,0,1:T(8,128)(2,1)}), bf16[48,32,512]{2,0,1:T(8,128)(2,1)}, u32[]{:S(2)}, u32[]{:S(2)}) %all-to-all-start.1) | async-done | bytes 1572896 | tf_op jit(solution)/shard_map/all_to_all | solution.py:43
  111.8 2.0 convolution_bitcast_fusion.1
  113.8 1.0 slice_add_fusion.2
  114.8 0.2 all-reduce.8.cloned.1.call-start
  115.1 129.5 %all-reduce.6.cloned.1.call-done = f32[1536,128]{0,1:T(8,128)} async-done(((f32[1536,128]{0,1:T(8,128)}), f32[1536,128]{0,1:T(8,128)}) %all-reduce.6.cloned.1.call-update) | async-done | bytes 786448 | tf_op jit(solution)/shard_map/psum | solution.py:71
  244.7 2.2 fusion.23
  246.9 0.1 copy.33
  247.0 11.7 %cholesky.59 = f32[128,128]{1,0:T(8,128)S(1)} custom-call(f32[128,128]{1,0:T(8,128)S(1)} %fusion.66), custom_call_target="Cholesky" | custom-call | tf_op jit(solution)/shard_map/jit(cholesky)/cholesky | solution.py:35
  258.7 0.6 compare_reduce_fusion.2
  259.4 0.7 fusion.58
  260.0 9.8 %custom-call.11 = f32[1,128,128]{1,2,0:T(8,128)S(1)} custom-call(f32[1,128,128]{2,1,0:T(8,128)S(1)} %fusion.58), custom_call_target="InvertDiagBlocksLowerTriangular" | custom-call | tf_op jit(solution)/shard_map/jit(_solve_triangular)/triangular_solve | solution.py:36
  269.9 2.0 reduce-precision_convert_fusion.3
  271.8 2.0 convolution_bitcast_fusion.5
  273.9 0.5 fusion.57
  274.4 0.5 convolution_add_fusion
  275.0 1.4 collective-permute-start.2
  276.5 1.3 collective-permute-start.3
  277.8 3.6 collective-permute-done.3
  281.4 0.7 convolution_bitcast_fusion.2
  282.2 1.1 slice_add_fusion
  283.3 0.3 all-reduce.10.cloned.1.call-start
  283.5 136.5 %all-reduce.8.cloned.1.call-done = f32[2048,128]{0,1:T(8,128)} async-done(((f32[2048,128]{0,1:T(8,128)}), f32[2048,128]{0,1:T(8,128)}) %all-reduce.8.cloned.1.call-update) | async-done | bytes 1048592 | tf_op jit(solution)/shard_map/psum | solution.py:83
  420.0 2.7 fusion.11
  422.7 0.1 copy.34
  422.8 11.7 %cholesky.70 = f32[128,128]{1,0:T(8,128)S(1)} custom-call(f32[128,128]{1,0:T(8,128)S(1)} %fusion.64), custom_call_target="Cholesky" | custom-call | tf_op jit(solution)/shard_map/jit(cholesky)/cholesky | solution.py:35
  434.6 0.6 compare_reduce_fusion.1
  435.2 0.7 fusion.59
  435.9 9.8 %custom-call.9 = f32[1,128,128]{1,2,0:T(8,128)S(1)} custom-call(f32[1,128,128]{2,1,0:T(8,128)S(1)} %fusion.59), custom_call_target="InvertDiagBlocksLowerTriangular" | custom-call | tf_op jit(solution)/shard_map/jit(_solve_triangular)/triangular_solve | solution.py:36
  445.7 2.0 reduce-precision_convert_fusion.1
  447.7 0.7 convolution_bitcast_fusion.4
  448.5 1.3 collective-permute-start.4
  449.8 1.5 collective-permute-start.5
  451.4 3.3 collective-permute-done.5
  454.8 0.5 fusion.41
  455.3 0.5 convolution_add_fusion.1
  455.9 2.0 convolution_bitcast_fusion
  458.0 1.0 slice_add_fusion.1
  459.0 0.9 copy-done.3
  459.9 1.2 fusion.27
  461.0 133.8 %all-reduce.10.cloned.1.call-done = f32[1536,128]{0,1:T(8,128)} async-done(((f32[1536,128]{0,1:T(8,128)}), f32[1536,128]{0,1:T(8,128)}) %all-reduce.10.cloned.1.call-update) | async-done | bytes 786448 | tf_op jit(solution)/shard_map/psum | solution.py:71
  594.9 2.2 fusion.20
  597.2 11.7 %cholesky.81 = f32[128,128]{1,0:T(8,128)S(1)} custom-call(f32[128,128]{1,0:T(8,128)S(1)} %fusion.62), custom_call_target="Cholesky" | custom-call | tf_op jit(solution)/shard_map/jit(cholesky)/cholesky | solution.py:35
  608.9 0.6 compare_reduce_fusion
  609.6 0.7 fusion.60
  610.2 9.8 %custom-call.12 = f32[1,128,128]{1,2,0:T(8,128)S(1)} custom-call(f32[1,128,128]{2,1,0:T(8,128)S(1)} %fusion.60), custom_call_target="InvertDiagBlocksLowerTriangular" | custom-call | tf_op jit(solution)/shard_map/jit(_solve_triangular)/triangular_solve | solution.py:36
  620.1 2.0 convolution_convert_fusion
  622.0 2.5 fusion.92
  (52 shorter events, 1.3 us)
Async XLA Ops:
  12.0 57.4 %all-to-all-start = ((bf16[64,32,512]{2,0,1:T(8,128)(2,1)}), bf16[64,32,512]{2,0,1:T(8,128)(2,1)S(1)}, u32[]{:S(2)}, u32[]{:S(2)}) async-start(bf16[64,32,512]{2,0,1:T(8,128)(2,1)} %copy.31), calls=%async_computation | async-start | bytes 4194304 | tf_op jit(solution)/shard_map/all_to_all | solution.py:42
  21.3 2.0 copy-start.6
  23.3 49.7 %copy-start.8 = (s32[4]{0:T(128)S(1)}, s32[4]{0:T(128)}, u32[]{:S(2)}) copy-start(s32[4]{0:T(128)} %param.13) | copy-start | bytes 52
  23.4 51.2 %copy-start.7 = (s32[4,4]{1,0:T(4,128)S(1)}, s32[4,4]{1,0:T(4,128)}, u32[]{:S(2)}) copy-start(s32[4,4]{1,0:T(4,128)} %param.17) | copy-start | bytes 196
  69.4 6.6 %copy-start = (bf16[64,32,512]{2,0,1:T(8,128)(2,1)}, bf16[64,32,512]{2,0,1:T(8,128)(2,1)S(1)}, u32[]{:S(2)}) copy-start(bf16[64,32,512]{2,0,1:T(8,128)(2,1)S(1)} %all-to-all-done) | copy-start | bytes 6291460
  69.4 42.4 %all-to-all-start.1 = ((bf16[48,32,512]{2,0,1:T(8,128)(2,1)}), bf16[48,32,512]{2,0,1:T(8,128)(2,1)}, u32[]{:S(2)}, u32[]{:S(2)}) async-start(bf16[48,32,512]{2,0,1:T(8,128)(2,1)} %copy.32), calls=%async_computation.1 | async-start | bytes 3145728 | tf_op jit(solution)/shard_map/all_to_all | solution.py:43
  72.9 171.7 %all-reduce.6.cloned.1.call-start = ((), (), s32[]{:S(2)}) async-start(), calls=%async_computation.2 | async-start | bytes 1572864 | tf_op jit(solution)/shard_map/psum | solution.py:71
  76.8 4.2 collective-permute-start
  78.8 4.4 collective-permute-start.1
  113.8 1.2 copy-start.9
  114.8 305.2 %all-reduce.8.cloned.1.call-start = ((), (), s32[]{:S(2)}) async-start(), calls=%async_computation.3 | async-start | bytes 2097152 | tf_op jit(solution)/shard_map/psum | solution.py:83
  274.9 6.5 %copy-start.1 = (bf16[64,32,512]{2,0,1:T(8,128)(2,1)S(1)}, bf16[64,32,512]{2,0,1:T(8,128)(2,1)}, u32[]{:S(2)}) copy-start(bf16[64,32,512]{2,0,1:T(8,128)(2,1)} %copy-done) | copy-start | bytes 6291460
  275.0 2.7 collective-permute-start.2
  276.5 4.9 collective-permute-start.3
  283.3 311.6 %all-reduce.10.cloned.1.call-start = ((), (), s32[]{:S(2)}) async-start(), calls=%async_computation.4 | async-start | bytes 1572864 | tf_op jit(solution)/shard_map/psum | solution.py:71
  420.0 25.7 %copy-start.4 = (f32[2048,128]{0,1:T(8,128)S(1)}, f32[2048,128]{0,1:T(8,128)}, u32[]{:S(2)}) copy-start(f32[2048,128]{0,1:T(8,128)} %all-reduce.8.cloned.1.call-done) | copy-start | bytes 3145732
  445.7 2.0 copy-start.2
  448.5 2.9 collective-permute-start.4
  449.8 4.9 collective-permute-start.5
  457.9 1.9 copy-start.3
  457.9 1.9 copy-start.5
Sparse Core Ops, SparseCore 0:
  114.9 129.6 all-reduce.5
  283.4 136.5 all-reduce.7
  459.1 135.7 all-reduce.9

commit v2 on v1

--- a/solution.py
+++ b/solution.py
@@ -1,6 +1,10 @@
+import functools
+
 import jax
 import jax.numpy as jnp
 from jax import lax
+from jax.experimental import pallas as pl
+from jax.experimental.pallas import tpu as pltpu
 from jax.sharding import PartitionSpec as P
 
 REACH = 2
@@ -28,6 +32,117 @@
 def live(counts, slots):
     inner = jnp.arange(slots, dtype=jnp.int32)
     return (inner[None, :] < counts[:, None]).reshape(-1, 1)
+
+
+MESH = pl.DeviceIdType.MESH
+
+
+def sum_kernel(shifts, members, part_ref, out_ref, total, landing, send_sem, recv_sem):
+    group = lax.axis_index("shift")
+    member = lax.axis_index("rows")
+    pairs = members // 2
+    core = lax.rem(member, 2)
+    pair = member // 2
+
+    def core_peer(step):
+        return (group, pair * 2 + lax.rem(core + step, 2))
+
+    def shift_peer(step):
+        return (lax.rem(group + step, shifts), member)
+
+    def pair_peer(step):
+        return (group, lax.rem(pair + step, pairs) * 2 + core)
+
+    stages = [(2, core, core_peer), (shifts, group, shift_peer), (pairs, pair, pair_peer)]
+    stages = [stage for stage in stages if stage[0] > 1]
+
+    barrier = pltpu.get_barrier_semaphore()
+    peers = 0
+    for size, _, peer in stages:
+        for step in range(1, size):
+            pl.semaphore_signal(barrier, inc=1, device_id=peer(step), device_id_type=MESH)
+            peers += 1
+    pl.semaphore_wait(barrier, peers)
+
+    rows = part_ref.shape[0]
+    length = rows
+    start = 0
+    used = 0
+    place = 0
+    source = part_ref
+    spans = []
+    for size, position, peer in stages:
+        piece = length // size
+        copies = []
+        for step in range(1, size):
+            target = start + lax.rem(position + step, size) * piece
+            copy = pltpu.make_async_remote_copy(
+                src_ref=source.at[pl.ds(pl.multiple_of(target, 8), piece)],
+                dst_ref=landing.at[pl.ds(place + (step - 1) * piece, piece)],
+                send_sem=send_sem.at[used],
+                recv_sem=recv_sem.at[used],
+                device_id=peer(step),
+                device_id_type=MESH,
+            )
+            copy.start()
+            copies.append(copy)
+            used += 1
+        start = start + position * piece
+        mine = pl.ds(pl.multiple_of(start, 8), piece)
+        for copy in copies:
+            copy.wait()
+        value = source[mine]
+        for step in range(1, size):
+            value = value + landing[pl.ds(place + (step - 1) * piece, piece)]
+        length = piece
+        place += (size - 1) * piece
+        spans.append((mine, size, peer))
+        if len(spans) == len(stages):
+            out_ref[mine] = value
+        else:
+            total[mine] = value
+            source = total
+    for mine, size, peer in reversed(spans):
+        copies = []
+        for step in range(1, size):
+            copy = pltpu.make_async_remote_copy(
+                src_ref=out_ref.at[mine],
+                dst_ref=out_ref.at[mine],
+                send_sem=send_sem.at[used],
+                recv_sem=recv_sem.at[used],
+                device_id=peer(step),
+                device_id_type=MESH,
+            )
+            copy.start()
+            copies.append(copy)
+            used += 1
+        for copy in copies:
+            copy.wait()
+
+
+def summed(part, call):
+    shifts, members = lax.axis_size("shift"), lax.axis_size("rows")
+    rows = part.shape[0]
+    step = 8 * shifts * members
+    padded = -(-rows // step) * step
+    if padded > rows:
+        part = jnp.pad(part, ((0, padded - rows), (0, 0)))
+    copies = 2 * (1 + shifts - 1 + members // 2 - 1)
+    total = pl.pallas_call(
+        functools.partial(sum_kernel, shifts, members),
+        out_shape=jax.ShapeDtypeStruct(part.shape, F32),
+        in_specs=[pl.BlockSpec(memory_space=pltpu.VMEM)],
+        out_specs=pl.BlockSpec(memory_space=pltpu.VMEM),
+        scratch_shapes=[
+            pltpu.VMEM(part.shape, F32),
+            pltpu.VMEM(part.shape, F32),
+            pltpu.SemaphoreType.DMA((copies,)),
+            pltpu.SemaphoreType.DMA((copies,)),
+        ],
+        compiler_params=pltpu.CompilerParams(collective_id=call, has_side_effects=True),
+        name="summed%d" % call,
+    )(part)
+    return total[:rows]
 
 
 def orth_local(matrix):
@@ -61,16 +176,16 @@
     edge = REACH * size
     width = omega.shape[1]
 
-    def forward(right):
+    def forward(right, call):
         rows = joined(dot(zc, split(right), 0, 0))
         before = lax.ppermute(rows[-edge:], AXES, up)
         after = lax.ppermute(rows[:edge], AXES, down)
         wide = split(jnp.concatenate([before, rows, after], axis=0))
         mixed = joined(dot(banded, wide, 1, 0) + dot(banded_rest, wide, 1, 0))
         part = joined(dot(zo, split(mixed), 1, 0))
-        return jnp.where(live_o, lax.psum(part, AXES), 0.0)
-
-    def backward(left):
+        return jnp.where(live_o, summed(part, call), 0.0)
+
+    def backward(left, call):
         rows = dot(zo, split(left), 0, 0)
         rows = split(joined(rows))
         wide = joined(dot(banded, rows, 0, 0) + dot(banded_rest, rows, 0, 0))
@@ -80,12 +195,12 @@
         rows = rows + jnp.pad(above, ((0, rows.shape[0] - edge), (0, 0)))
         rows = rows + jnp.pad(below, ((rows.shape[0] - edge, 0), (0, 0)))
         part = joined(dot(zc, split(rows), 1, 0))
-        return jnp.where(live_c, lax.psum(part, AXES), 0.0)
-
-    first = orth_local(forward(jnp.where(live_c, omega, 0.0)))
-    right = orth_local(backward(first))
+        return jnp.where(live_c, summed(part, call), 0.0)
+
+    first = orth_local(forward(jnp.where(live_c, omega, 0.0), 0))
+    right = orth_local(backward(first, 1))
     proj_c = dot(right.astype(BF16), zc, 0, 0)
-    left = orth_local(forward(right))
+    left = orth_local(forward(right, 2))
     proj_o = dot(left.astype(BF16), zo, 0, 0)
     return (proj_c, proj_o)
 

time: 638 us -> 323 us (0.51)
  waiting for transfers between devices: 482 us -> 79.9 us
  Pallas kernels: 0 us -> 99.4 us
  between operations: 14.7 us -> 1.62 us
    psum x3 -> x0, waiting for transfers between devices: 400 us -> none  [the longest x2 263 us: forward(): return jnp.where(live_o, lax.psum(part, AXES), 0.0)]
    pallas_call x0 -> x3, Pallas kernels: none -> 99.4 us  [summed(): pl.pallas_call(functools.partial(sum_kernel, shifts, members), out_shape=...]
  transfers between devices with their start and end apart: 11 -> 8, of which waited for: 8 -> 5; matrix products, arithmetic and copies ran while one was open for 2% -> 3% of each run, Pallas kernels for 0% -> 0%
where the time goes in v2:
time: 323 us; the launch traced here: 318 us
  Pallas kernels  99.4 us (31%)
  waiting for transfers between devices  79.9 us (25%)
  other arithmetic  73.7 us (23%)
  matrix products  31.6 us (10%)
  starting transfers between devices  21.7 us (7%)
  local copies, waits for them, and re-layouts  9.82 us (3%)
    pallas_call x3, Pallas kernels, summed(): pl.pallas_call(functools.partial(sum_kernel, shifts, members), out_shape=...  99.4 us
    all_to_all x1, waiting for transfers between devices, per_device(): zc = lax.all_to_all(zc_in[0], AXES, split_axis=1, concat_axis=0, tiled=True)  45.9 us
    another operation x9, other arithmetic, orth_local(): lower = jnp.linalg.cholesky(square)  37.2 us
    another operation x6, other arithmetic, orth_local(): return jax.scipy.linalg.solve_triangular(lower, matrix.T, lower=True).T  31.4 us
    all_to_all x1, waiting for transfers between devices, per_device(): zo = lax.all_to_all(zo_in[0], AXES, split_axis=1, concat_axis=0, tiled=True)  28.4 us
    dot_general x14, matrix products, dot(): lax.dot_general(left, right, (((contract_left,), (contract_right,)), ((),...  15.2 us
    dot_general x3, matrix products, orth_local(): square = jnp.dot(matrix.T, matrix, precision=lax.Precision.HIGHEST)  10.5 us
    all_to_all x1, starting transfers between devices, per_device(): zc = lax.all_to_all(zc_in[0], AXES, split_axis=1, concat_axis=0, tiled=True)  7.3 us
  transfers between devices with their start and end apart: 8, of which 5 were waited for; matrix products, arithmetic and copies ran while one was open for 3% of the time, Pallas kernels for 0%

profile of v2, /device:TPU:0, one launch (start us, length us, event | category | flops | bytes accessed | tf_op | source)
XLA Modules:
  0.0 317.8 jit_solution(15714610615776937555)
XLA Ops:
  0.6 2.4 copy.51
  3.0 2.5 copy.38
  5.5 7.3 %all-to-all-start = ((bf16[64,32,512]{2,0,1:T(8,128)(2,1)}), bf16[64,32,512]{2,0,1:T(8,128)(2,1)S(1)}, u32[]{:S(2)}, u32[]{:S(2)}) async-start(bf16[64,32,512]{2,0,1:T(8,128)(2,1)} %copy.38), calls=%async_computation | async-start | bytes 4194304 | tf_op jit(solution)/shard_map/all_to_all | solution.py:157
  12.8 2.0 copy.52
  14.8 2.0 copy.39
  17.0 45.9 %all-to-all-done = bf16[64,32,512]{2,0,1:T(8,128)(2,1)S(1)} async-done(((bf16[64,32,512]{2,0,1:T(8,128)(2,1)}), bf16[64,32,512]{2,0,1:T(8,128)(2,1)S(1)}, u32[]{:S(2)}, u32[]{:S(2)}) %all-to-all-start) | async-done | bytes 2097184 | tf_op jit(solution)/shard_map/all_to_all | solution.py:157
  62.9 3.5 %all-to-all-start.1 = ((bf16[48,32,512]{2,0,1:T(8,128)(2,1)}), bf16[48,32,512]{2,0,1:T(8,128)(2,1)}, u32[]{:S(2)}, u32[]{:S(2)}) async-start(bf16[48,32,512]{2,0,1:T(8,128)(2,1)} %copy.39), calls=%async_computation.1 | async-start | bytes 3145728 | tf_op jit(solution)/shard_map/all_to_all | solution.py:158
  66.6 0.9 select_reduce_fusion
  67.5 0.2 copy-done.5
  67.7 0.3 reduce-precision_convert_fusion.2
  68.1 0.4 copy-done.1
  68.4 0.7 convolution_bitcast_fusion.6
  69.2 2.0 collective-permute-start
  71.2 1.5 collective-permute-start.1
  72.8 2.9 collective-permute-done.1
  75.6 0.1 reduce-precision_convert_fusion.5
  75.7 0.5 fusion.42
  76.2 0.5 convolution_add_fusion.2
  76.8 28.4 %all-to-all-done.1 = bf16[48,32,512]{2,0,1:T(8,128)(2,1)} async-done(((bf16[48,32,512]{2,0,1:T(8,128)(2,1)}), bf16[48,32,512]{2,0,1:T(8,128)(2,1)}, u32[]{:S(2)}, u32[]{:S(2)}) %all-to-all-start.1) | async-done | bytes 1572896 | tf_op jit(solution)/shard_map/all_to_all | solution.py:158
  105.2 2.0 convolution_bitcast_fusion.1
  107.3 0.9 slice_add_fusion.2.part_ref
  108.2 28.1 %summed0.1 = f32[1536,128]{1,0:T(8,128)} custom-call(f32[1536,128]{1,0:T(8,128)} %slice_add_fusion.2.part_ref), custom_call_target="tpu_custom_call" | custom-call | tf_op jit(solution)/shard_map/summed0/pallas_call | solution.py:131
  136.4 3.2 %fusion.23 = f32[128,128]{1,0:T(8,128)S(1)} fusion(f32[1536,128]{1,0:T(8,128)} %summed0.1, pred[1536]{0:T(1024)(128)(4,1)S(1)} %lt.68), kind=kOutput, calls=%fused_computation.50 | convolution fusion | flops 302186496 | bytes 853504 | tf_op jit(solution)/shard_map/dot_general | solution.py:149
  139.6 0.1 copy.41
  139.7 11.7 %cholesky.59 = f32[128,128]{1,0:T(8,128)S(1)} custom-call(f32[128,128]{1,0:T(8,128)S(1)} %fusion.66), custom_call_target="Cholesky" | custom-call | tf_op jit(solution)/shard_map/jit(cholesky)/cholesky | solution.py:150
  151.4 0.6 compare_reduce_fusion.2
  152.1 0.7 fusion.58
  152.8 9.8 %custom-call.11 = f32[1,128,128]{1,2,0:T(8,128)S(1)} custom-call(f32[1,128,128]{2,1,0:T(8,128)S(1)} %fusion.58), custom_call_target="InvertDiagBlocksLowerTriangular" | custom-call | tf_op jit(solution)/shard_map/jit(_solve_triangular)/triangular_solve | solution.py:151
  162.6 2.2 reduce-precision_convert_fusion.3
  164.8 2.0 convolution_bitcast_fusion.5
  166.8 0.5 fusion.57
  167.3 0.8 convolution_add_fusion
  168.2 2.4 collective-permute-start.2
  170.6 1.3 collective-permute-start.3
  171.9 2.0 collective-permute-done.3
  174.0 0.7 convolution_bitcast_fusion.2
  174.7 1.1 slice_add_fusion.part_ref
  175.8 36.8 %summed1.1 = f32[2048,128]{1,0:T(8,128)} custom-call(f32[2048,128]{1,0:T(8,128)} %slice_add_fusion.part_ref), custom_call_target="tpu_custom_call" | custom-call | tf_op jit(solution)/shard_map/summed1/pallas_call | solution.py:131
  212.7 4.0 %fusion.11 = f32[128,128]{1,0:T(8,128)S(1)} fusion(f32[2048,128]{1,0:T(8,128)} %summed1.1, pred[2048]{0:T(1024)(128)(4,1)S(1)} %bitcast.104), kind=kOutput, calls=%fused_computation.32 | convolution fusion | flops 402915328 | bytes 1116160 | tf_op jit(solution)/shard_map/dot_general | solution.py:149
  216.7 0.1 copy.43
  216.8 11.7 %cholesky.70 = f32[128,128]{1,0:T(8,128)S(1)} custom-call(f32[128,128]{1,0:T(8,128)S(1)} %fusion.64), custom_call_target="Cholesky" | custom-call | tf_op jit(solution)/shard_map/jit(cholesky)/cholesky | solution.py:150
  228.6 0.6 compare_reduce_fusion.1
  229.2 0.7 fusion.59
  229.9 9.8 %custom-call.9 = f32[1,128,128]{1,2,0:T(8,128)S(1)} custom-call(f32[1,128,128]{2,1,0:T(8,128)S(1)} %fusion.59), custom_call_target="InvertDiagBlocksLowerTriangular" | custom-call | tf_op jit(solution)/shard_map/jit(_solve_triangular)/triangular_solve | solution.py:151
  239.7 1.6 reduce-precision_convert_fusion.1
  241.3 0.7 convolution_bitcast_fusion.4
  242.1 2.3 collective-permute-start.4
  244.4 1.5 collective-permute-start.5
  245.9 1.2 fusion.27
  247.1 0.7 collective-permute-done.5
  247.8 0.1 reduce-precision_convert_fusion.4
  247.9 0.5 fusion.41
  248.4 0.5 convolution_add_fusion.1
  249.0 2.0 convolution_bitcast_fusion
  251.0 1.0 slice_add_fusion.1.part_ref
  252.0 34.5 %summed2.1 = f32[1536,128]{1,0:T(8,128)} custom-call(f32[1536,128]{1,0:T(8,128)} %slice_add_fusion.1.part_ref), custom_call_target="tpu_custom_call" | custom-call | tf_op jit(solution)/shard_map/summed2/pallas_call | solution.py:131
  286.5 3.2 %fusion.20 = f32[128,128]{1,0:T(8,128)S(1)} fusion(f32[1536,128]{1,0:T(8,128)} %summed2.1, pred[1536]{0:T(1024)(128)(4,1)S(1)} %lt.68), kind=kOutput, calls=%fused_computation.47 | convolution fusion | flops 302186496 | bytes 853504 | tf_op jit(solution)/shard_map/dot_general | solution.py:149
  289.7 0.1 copy.45
  289.8 11.7 %cholesky.81 = f32[128,128]{1,0:T(8,128)S(1)} custom-call(f32[128,128]{1,0:T(8,128)S(1)} %fusion.62), custom_call_target="Cholesky" | custom-call | tf_op jit(solution)/shard_map/jit(cholesky)/cholesky | solution.py:150
  301.6 0.6 compare_reduce_fusion
  302.2 0.7 fusion.60
  302.9 9.8 %custom-call.12 = f32[1,128,128]{1,2,0:T(8,128)S(1)} custom-call(f32[1,128,128]{2,1,0:T(8,128)S(1)} %fusion.60), custom_call_target="InvertDiagBlocksLowerTriangular" | custom-call | tf_op jit(solution)/shard_map/jit(_solve_triangular)/triangular_solve | solution.py:151
  312.7 2.2 convolution_convert_fusion
  314.9 2.5 fusion.92
  (47 shorter events, 1.0 us)
Async XLA Ops:
  5.5 57.4 %all-to-all-start = ((bf16[64,32,512]{2,0,1:T(8,128)(2,1)}), bf16[64,32,512]{2,0,1:T(8,128)(2,1)S(1)}, u32[]{:S(2)}, u32[]{:S(2)}) async-start(bf16[64,32,512]{2,0,1:T(8,128)(2,1)} %copy.38), calls=%async_computation | async-start | bytes 4194304 | tf_op jit(solution)/shard_map/all_to_all | solution.py:157
  14.8 2.1 copy-start.7
  14.8 2.1 copy-start.8
  16.8 49.6 %copy-start.9 = (s32[4]{0:T(128)S(1)}, s32[4]{0:T(128)}, u32[]{:S(2)}) copy-start(s32[4]{0:T(128)} %param.13) | copy-start | bytes 52
  16.8 49.7 %copy-start.6 = (bf16[4,4,128,128]{3,2,1,0:T(8,128)(2,1)S(1)}, bf16[4,4,128,128]{3,2,1,0:T(8,128)(2,1)}, u32[]{:S(2)}) copy-start(bf16[4,4,128,128]{3,2,1,0:T(8,128)(2,1)} %param.15) | copy-start | bytes 1572868
  62.9 3.6 %copy-start = (bf16[64,32,512]{2,0,1:T(8,128)(2,1)}, bf16[64,32,512]{2,0,1:T(8,128)(2,1)S(1)}, u32[]{:S(2)}) copy-start(bf16[64,32,512]{2,0,1:T(8,128)(2,1)S(1)} %all-to-all-done) | copy-start | bytes 6291460
  62.9 42.3 %all-to-all-start.1 = ((bf16[48,32,512]{2,0,1:T(8,128)(2,1)}), bf16[48,32,512]{2,0,1:T(8,128)(2,1)}, u32[]{:S(2)}, u32[]{:S(2)}) async-start(bf16[48,32,512]{2,0,1:T(8,128)(2,1)} %copy.39), calls=%async_computation.1 | async-start | bytes 3145728 | tf_op jit(solution)/shard_map/all_to_all | solution.py:158
  66.5 1.2 copy-start.5
  66.6 1.9 copy-start.1
  68.4 4.2 %copy-start.10 = (s32[4]{0:T(128)S(1)}, s32[4]{0:T(128)}, u32[]{:S(2)}) copy-start(s32[4]{0:T(128)} %param.14) | copy-start | bytes 52
  69.2 3.5 %collective-permute-start = (f32[256,128]{0,1:T(8,128)S(1)}, f32[256,128]{0,1:T(8,128)S(1)}, u32[]{:S(2)}, u32[]{:S(2)}) collective-permute-start(f32[256,128]{0,1:T(8,128)S(1)} %get-tuple-element.26), channel_id=1, source_target_pairs={{0,1},{1,2},{2,3},{3,4},{4,5},{5,6},{6,7},{7,8},{8,9},{9,10},{10,1... | collective-permute-start | bytes 393224 | tf_op jit(solution)/shard_map/ppermute | solution.py:181
  71.2 4.4 %collective-permute-start.1 = (f32[256,128]{0,1:T(8,128)S(1)}, f32[256,128]{0,1:T(8,128)S(1)}, u32[]{:S(2)}, u32[]{:S(2)}) collective-permute-start(f32[256,128]{0,1:T(8,128)S(1)} %get-tuple-element.27), channel_id=1, source_target_pairs={{1,0},{2,1},{3,2},{4,3},{5,4},{6,5},{7,6},{8,7},{9,8},{10,9},{11,1... | collective-permute-start | bytes 393224 | tf_op jit(solution)/shard_map/ppermute | solution.py:182
  168.1 5.9 %copy-start.2 = (bf16[64,32,512]{2,0,1:T(8,128)(2,1)S(1)}, bf16[64,32,512]{2,0,1:T(8,128)(2,1)}, u32[]{:S(2)}) copy-start(bf16[64,32,512]{2,0,1:T(8,128)(2,1)} %copy-done) | copy-start | bytes 6291460
  168.2 3.7 %collective-permute-start.2 = (f32[256,128]{0,1:T(8,128)S(1)}, f32[256,128]{0,1:T(8,128)S(1)}, u32[]{:S(2)}, u32[]{:S(2)}) collective-permute-start(f32[256,128]{0,1:T(8,128)S(1)} %get-tuple-element.16), channel_id=1, source_target_pairs={{0,1},{1,2},{2,3},{3,4},{4,5},{5,6},{6,7},{7,8},{8,9},{9,10},{10,1... | collective-permute-start | bytes 393224 | tf_op jit(solution)/shard_map/ppermute | solution.py:192
  170.6 3.3 %collective-permute-start.3 = (f32[256,128]{0,1:T(8,128)S(1)}, f32[256,128]{0,1:T(8,128)S(1)}, u32[]{:S(2)}, u32[]{:S(2)}) collective-permute-start(f32[256,128]{0,1:T(8,128)S(1)} %get-tuple-element.17), channel_id=1, source_target_pairs={{1,0},{2,1},{3,2},{4,3},{5,4},{6,5},{7,6},{8,7},{9,8},{10,9},{11,1... | collective-permute-start | bytes 393224 | tf_op jit(solution)/shard_map/ppermute | solution.py:193
  212.7 27.0 %copy-start.4 = (f32[2048,128]{1,0:T(8,128)S(1)}, f32[2048,128]{1,0:T(8,128)}, u32[]{:S(2)}) copy-start(f32[2048,128]{1,0:T(8,128)} %summed1.1) | copy-start | bytes 3145732
  239.7 1.6 copy-start.3
  242.1 5.0 %collective-permute-start.4 = (f32[256,128]{0,1:T(8,128)S(1)}, f32[256,128]{0,1:T(8,128)S(1)}, u32[]{:S(2)}, u32[]{:S(2)}) collective-permute-start(f32[256,128]{0,1:T(8,128)S(1)} %get-tuple-element.24), channel_id=1, source_target_pairs={{0,1},{1,2},{2,3},{3,4},{4,5},{5,6},{6,7},{7,8},{8,9},{9,10},{10,1... | collective-permute-start | bytes 393224 | tf_op jit(solution)/shard_map/ppermute | solution.py:181
  244.4 3.4 %collective-permute-start.5 = (f32[256,128]{0,1:T(8,128)S(1)}, f32[256,128]{0,1:T(8,128)S(1)}, u32[]{:S(2)}, u32[]{:S(2)}) collective-permute-start(f32[256,128]{0,1:T(8,128)S(1)} %get-tuple-element.25), channel_id=1, source_target_pairs={{1,0},{2,1},{3,2},{4,3},{5,4},{6,5},{7,6},{8,7},{9,8},{10,9},{11,1... | collective-permute-start | bytes 393224 | tf_op jit(solution)/shard_map/ppermute | solution.py:182

commit v3 on v2

--- a/solution.py
+++ b/solution.py
@@ -37,10 +37,31 @@
 MESH = pl.DeviceIdType.MESH
 
 
-def sum_kernel(shifts, members, part_ref, out_ref, total, landing, send_sem, recv_sem):
+def halved(matrix):
+    high = matrix.astype(BF16)
+    return high, (matrix - high.astype(F32)).astype(BF16)
+
+
+def times(left, right):
+    high, rest = halved(right)
+    return dot(left, high, 1, 0) + dot(left, rest, 1, 0)
+
+
+def sum_kernel(shifts, members, kind, edge, rows_ref, *refs):
+    if kind == "forward":
+        banded_ref, rest_ref, factor_ref, live_ref = refs[:4]
+    else:
+        factor_ref, live_ref = refs[:2]
+    out_ref, part_ref, total, landing, halo, send_sem, recv_sem, halo_send, halo_recv = refs[-9:]
     group = lax.axis_index("shift")
     member = lax.axis_index("rows")
     pairs = members // 2
+    devices = shifts * members
+    index = group * members + member
+    sides = []
+    for step in (1, devices - 1):
+        beside = lax.rem(index + step, devices)
+        sides.append((beside // members, lax.rem(beside, members)))
     core = lax.rem(member, 2)
     pair = member // 2
 
@@ -62,7 +83,39 @@
         for step in range(1, size):
             pl.semaphore_signal(barrier, inc=1, device_id=peer(step), device_id_type=MESH)
             peers += 1
-    pl.semaphore_wait(barrier, peers)
+    for side in sides:
+        pl.semaphore_signal(barrier, inc=1, device_id=side, device_id_type=MESH)
+    pl.semaphore_wait(barrier, peers + 2)
+
+    depth = rows_ref.shape[0]
+    halos = []
+    for n, first in ((0, depth - edge), (1, 0)):
+        copy = pltpu.make_async_remote_copy(
+            src_ref=rows_ref.at[pl.ds(first, edge)],
+            dst_ref=halo.at[n],
+            send_sem=halo_send.at[n],
+            recv_sem=halo_recv.at[n],
+            device_id=sides[n],
+            device_id_type=MESH,
+        )
+        copy.start()
+        halos.append(copy)
+    for copy in halos:
+        copy.wait()
+    if kind == "forward":
+        wide = jnp.concatenate([halo[0], rows_ref[...], halo[1]], axis=0)
+        mixed = times(banded_ref[...], wide) + times(rest_ref[...], wide)
+    else:
+        kept = rows_ref[pl.ds(edge, depth - 2 * edge), :]
+        blank = jnp.zeros((depth - 3 * edge, kept.shape[1]), F32)
+        mixed = kept + jnp.concatenate([halo[0], blank], axis=0)
+        mixed = mixed + jnp.concatenate([blank, halo[1]], axis=0)
+    count = factor_ref.shape[0]
+    part_ref[pl.ds(0, count), :] = times(factor_ref[...], mixed) * live_ref[...]
+    if part_ref.shape[0] > count:
+        part_ref[pl.ds(count, part_ref.shape[0] - count), :] = jnp.zeros(
+            (part_ref.shape[0] - count, part_ref.shape[1]), F32
+        )
 
     rows = part_ref.shape[0]
     length = rows
@@ -120,40 +173,95 @@
             copy.wait()
 
 
-def summed(part, call):
+def summed(kind, edge, call, rows, *others):
     shifts, members = lax.axis_size("shift"), lax.axis_size("rows")
-    rows = part.shape[0]
+    count, width = others[-1].shape[0], rows.shape[1]
     step = 8 * shifts * members
-    padded = -(-rows // step) * step
-    if padded > rows:
-        part = jnp.pad(part, ((0, padded - rows), (0, 0)))
+    shape = (-(-count // step) * step, width)
     copies = 2 * (1 + shifts - 1 + members // 2 - 1)
     total = pl.pallas_call(
-        functools.partial(sum_kernel, shifts, members),
-        out_shape=jax.ShapeDtypeStruct(part.shape, F32),
+        functools.partial(sum_kernel, shifts, members, kind, edge),
+        out_shape=jax.ShapeDtypeStruct(shape, F32),
+        in_specs=[pl.BlockSpec(memory_space=pltpu.VMEM)] * (1 + len(others)),
+        out_specs=pl.BlockSpec(memory_space=pltpu.VMEM),
+        scratch_shapes=[
+            pltpu.VMEM(shape, F32),
+            pltpu.VMEM(shape, F32),
+            pltpu.VMEM(shape, F32),
+            pltpu.VMEM((2, edge, width), F32),
+            pltpu.SemaphoreType.DMA((copies,)),
+            pltpu.SemaphoreType.DMA((copies,)),
+            pltpu.SemaphoreType.DMA((2,)),
+            pltpu.SemaphoreType.DMA((2,)),
+        ],
+        compiler_params=pltpu.CompilerParams(
+            collective_id=call, has_side_effects=True, vmem_limit_bytes=40 * 1024 * 1024
+        ),
+        name="summed%d" % call,
+    )(rows, *others)
+    return total[:count]
+
+
+def orth_kernel(matrix_ref, out_ref, square):
+    width = matrix_ref.shape[1]
+    high = lax.Precision.HIGHEST
+    matrix = matrix_ref[...]
+    square[...] = lax.dot_general(
+        matrix, matrix, (((0,), (0,)), ((), ())), precision=high, preferred_element_type=F32
+    )
+    lanes = lax.broadcasted_iota(jnp.int32, (8, width), 1)
+    below = lax.broadcasted_iota(jnp.int32, (8, width), 0)
+    panels = width // 8
+    groups = [square[8 * g : 8 * g + 8, :] for g in range(panels)]
+    for k in range(panels):
+        base = 8 * k
+        inside = (lanes >= base) & (lanes < base + 8)
+        columns = {
+            g: [jnp.broadcast_to(groups[g][:, base + j : base + j + 1], (8, width)) for j in range(8)]
+            for g in range(k, panels)
+        }
+        unit = jnp.where(lanes == below + base, 1.0, 0.0)
+        groups[k] = jnp.where(inside, unit, groups[k])
+        for g in range(k + 1, panels):
+            groups[g] = jnp.where(inside, 0.0, groups[g])
+        pivots = jnp.ones((8, width), F32)
+        for j in range(8):
+            own = columns[k]
+            pivot = jnp.broadcast_to(own[j][j : j + 1, :], (8, width))
+            inverse = 1.0 / pivot
+            pivots = jnp.where(below == j, pivot, pivots)
+            row = jnp.broadcast_to(groups[k][j : j + 1, :], (8, width))
+            heads = [
+                jnp.broadcast_to(own[n][j : j + 1, :], (8, width)) if n > j else None for n in range(8)
+            ]
+            for g in range(k, panels):
+                factor = columns[g][j] * inverse
+                if g == k:
+                    factor = jnp.where(below > j, factor, 0.0)
+                for n in range(j + 1, 8):
+                    columns[g][n] = columns[g][n] - factor * heads[n]
+                groups[g] = groups[g] - factor * row
+        done = jnp.where(lanes < base + 8, groups[k] * lax.rsqrt(pivots), 0.0)
+        square[base : base + 8, :] = done
+    out_ref[...] = lax.dot_general(
+        matrix_ref[...], square[...], (((1,), (1,)), ((), ())), precision=high, preferred_element_type=F32
+    )
+
+
+def orth_local(matrix):
+    width = matrix.shape[1]
+    return pl.pallas_call(
+        orth_kernel,
+        out_shape=jax.ShapeDtypeStruct(matrix.shape, F32),
         in_specs=[pl.BlockSpec(memory_space=pltpu.VMEM)],
         out_specs=pl.BlockSpec(memory_space=pltpu.VMEM),
-        scratch_shapes=[
-            pltpu.VMEM(part.shape, F32),
-            pltpu.VMEM(part.shape, F32),
-            pltpu.SemaphoreType.DMA((copies,)),
-            pltpu.SemaphoreType.DMA((copies,)),
-        ],
-        compiler_params=pltpu.CompilerParams(collective_id=call, has_side_effects=True),
-        name="summed%d" % call,
-    )(part)
-    return total[:rows]
-
-
-def orth_local(matrix):
-    square = jnp.dot(matrix.T, matrix, precision=lax.Precision.HIGHEST)
-    lower = jnp.linalg.cholesky(square)
-    return jax.scipy.linalg.solve_triangular(lower, matrix.T, lower=True).T
+        scratch_shapes=[pltpu.VMEM((width, width), F32)],
+        name="orth",
+    )(matrix)
 
 
 def per_device(zc_in, zo_in, count_c, count_o, mass, adjacency, ghost_len, omega):
     index = lax.axis_index(AXES)
-    devices = lax.axis_size(AXES)
     zc = lax.all_to_all(zc_in[0], AXES, split_axis=1, concat_axis=0, tiled=True)
     zo = lax.all_to_all(zo_in[0], AXES, split_axis=1, concat_axis=0, tiled=True)
     groups = count_c.shape[0]
@@ -171,31 +279,17 @@
     banded = lax.reduce_precision(dense, 8, 7)
     banded_rest = (dense - banded).astype(BF16)
     banded = banded.astype(BF16)
-    up = [(i, i + 1) for i in range(devices - 1)]
-    down = [(j, i) for i, j in up]
     edge = REACH * size
-    width = omega.shape[1]
 
     def forward(right, call):
         rows = joined(dot(zc, split(right), 0, 0))
-        before = lax.ppermute(rows[-edge:], AXES, up)
-        after = lax.ppermute(rows[:edge], AXES, down)
-        wide = split(jnp.concatenate([before, rows, after], axis=0))
-        mixed = joined(dot(banded, wide, 1, 0) + dot(banded_rest, wide, 1, 0))
-        part = joined(dot(zo, split(mixed), 1, 0))
-        return jnp.where(live_o, summed(part, call), 0.0)
+        return summed("forward", edge, call, rows, banded, banded_rest, zo, live_o.astype(F32))
 
     def backward(left, call):
         rows = dot(zo, split(left), 0, 0)
         rows = split(joined(rows))
         wide = joined(dot(banded, rows, 0, 0) + dot(banded_rest, rows, 0, 0))
-        above = lax.ppermute(wide[-edge:], AXES, up)
-        below = lax.ppermute(wide[:edge], AXES, down)
-        rows = wide[edge:-edge]
-        rows = rows + jnp.pad(above, ((0, rows.shape[0] - edge), (0, 0)))
-        rows = rows + jnp.pad(below, ((rows.shape[0] - edge, 0), (0, 0)))
-        part = joined(dot(zc, split(rows), 1, 0))
-        return jnp.where(live_c, summed(part, call), 0.0)
+        return summed("backward", edge, call, wide, zc, live_c.astype(F32))
 
     first = orth_local(forward(jnp.where(live_c, omega, 0.0), 0))
     right = orth_local(backward(first, 1))

time: 323 us -> 255 us (0.79); the launches traced: 318 us -> 254 us
  other arithmetic: 73.7 us -> 6.89 us
  Pallas kernels: 99.4 us -> 131 us
  matrix products: 31.6 us -> 8.33 us
  starting transfers between devices: 21.7 us -> 10.2 us
  local copies, waits for them, and re-layouts: 9.82 us -> 20.2 us
    another operation x15 -> x0, other arithmetic: 68.6 us -> none  [the longest x9 37.2 us: orth_local(): lower = jnp.linalg.cholesky(square)]
    pallas_call x3 -> x6, Pallas kernels: 99.4 us -> 131 us  [the longest x3 107 us: summed(): pl.pallas_call(functools.partial(sum_kernel, shifts, members, kind, edge)...]
    ppermute x6 -> x0, starting transfers between devices: 11 us -> none  [the longest x2 4.24 us: forward(): before = lax.ppermute(rows[-edge:], AXES, up)]
    unnamed x25 -> x43, local copies, waits for them, and re-layouts: 4.96 us -> 15.7 us
    dot_general x3 -> x0, matrix products: 10.5 us -> none  [orth_local(): square = jnp.dot(matrix.T, matrix, precision=lax.Precision.HIGHEST)]
    dot_general x14 -> x7, matrix products: 15.2 us -> 8.33 us  [dot(): lax.dot_general(left, right, (((contract_left,), (contract_right,)), ((),...]
    another operation x3 -> x0, matrix products: 5.97 us -> none  [orth_local(): return jax.scipy.linalg.solve_triangular(lower, matrix.T, lower=True).T]
    ppermute x6 -> x0, waiting for transfers between devices: 5.54 us -> none  [the longest x2 3.54 us: forward(): after = lax.ppermute(rows[:edge], AXES, down)]
  transfers between devices with their start and end apart: 8 -> 2, of which waited for: 5 -> 2; matrix products, arithmetic and copies ran while one was open for 3% -> 4% of each run, Pallas kernels for 0% -> 0%
where the time goes in v3:
time: 255 us; the launch traced here: 254 us
  Pallas kernels  131 us (51%)
  waiting for transfers between devices  76.9 us (30%)
  local copies, waits for them, and re-layouts  20.2 us (8%)
  starting transfers between devices  10.2 us (4%)
  matrix products  8.33 us (3%)
  other arithmetic  6.89 us (3%)
    pallas_call x3, Pallas kernels, summed(): pl.pallas_call(functools.partial(sum_kernel, shifts, members, kind, edge)...  107 us
    all_to_all x1, waiting for transfers between devices, per_device(): zc = lax.all_to_all(zc_in[0], AXES, split_axis=1, concat_axis=0, tiled=True)  46.1 us
    all_to_all x1, waiting for transfers between devices, per_device(): zo = lax.all_to_all(zo_in[0], AXES, split_axis=1, concat_axis=0, tiled=True)  30.7 us
    pallas_call x3, Pallas kernels, orth_local(): pl.pallas_call(orth_kernel, out_shape=jax.ShapeDtypeStruct(matrix.shape,...  24 us
    unnamed x43, local copies, waits for them, and re-layouts  15.7 us
    dot_general x7, matrix products, dot(): lax.dot_general(left, right, (((contract_left,), (contract_right,)), ((),...  8.33 us
    all_to_all x1, starting transfers between devices, per_device(): zc = lax.all_to_all(zc_in[0], AXES, split_axis=1, concat_axis=0, tiled=True)  7.3 us
  transfers between devices with their start and end apart: 2, of which 2 were waited for; matrix products, arithmetic and copies ran while one was open for 4% of the time, Pallas kernels for 0%

profile of v3, /device:TPU:0, one launch (start us, length us, event | category | flops | bytes accessed | tf_op | source)
XLA Modules:
  0.0 254.5 jit_solution(14758136460972395042)
XLA Ops:
  0.6 2.4 copy.32
  3.0 2.5 copy.21
  5.5 7.3 %all-to-all-start = ((bf16[64,32,512]{2,0,1:T(8,128)(2,1)}), bf16[64,32,512]{2,0,1:T(8,128)(2,1)S(1)}, u32[]{:S(2)}, u32[]{:S(2)}) async-start(bf16[64,32,512]{2,0,1:T(8,128)(2,1)} %copy.21), calls=%async_computation | async-start | bytes 4194304 | tf_op jit(solution)/shard_map/all_to_all | solution.py:265
  12.8 2.0 copy.33
  14.7 2.0 copy.23
  16.8 0.0 copy-start.17
  16.8 0.0 copy-start.16
  16.8 0.0 copy-start.13
  16.8 46.1 %all-to-all-done = bf16[64,32,512]{2,0,1:T(8,128)(2,1)S(1)} async-done(((bf16[64,32,512]{2,0,1:T(8,128)(2,1)}), bf16[64,32,512]{2,0,1:T(8,128)(2,1)S(1)}, u32[]{:S(2)}, u32[]{:S(2)}) %all-to-all-start) | async-done | bytes 2097184 | tf_op jit(solution)/shard_map/all_to_all | solution.py:265
  62.9 1.3 copy-done
  64.2 2.9 %all-to-all-start.1 = ((bf16[48,32,512]{2,0,1:T(8,128)(2,1)}), bf16[48,32,512]{2,0,1:T(8,128)(2,1)S(1)}, u32[]{:S(2)}, u32[]{:S(2)}) async-start(bf16[48,32,512]{2,0,1:T(8,128)(2,1)} %copy.23), calls=%async_computation.1 | async-start | bytes 3145728 | tf_op jit(solution)/shard_map/all_to_all | solution.py:266
  67.1 0.0 copy-done.17
  67.1 0.1 convert_bitcast_fusion
  67.2 0.0 copy-done.16
  67.2 0.1 convert_bitcast_fusion.1
  67.3 0.3 copy.35
  67.6 1.4 copy.37
  69.0 0.0 copy-done.14
  69.0 0.1 iota_compare_fusion.2
  69.1 0.0 copy-done.15
  69.1 0.1 iota_compare_fusion.1
  69.1 0.0 copy-done.13
  69.1 0.1 select_convert_fusion
  69.2 0.9 select_reduce_fusion
  70.1 0.0 copy-start.12
  70.2 1.6 fusion
  71.8 0.0 copy-done.12
  71.8 0.3 reduce-precision_convert_fusion.2
  72.1 1.2 copy-done.1
  73.4 0.9 convolution_bitcast_fusion.2
  74.3 0.7 slice_add_fusion.3.rows_ref
  75.0 30.7 %all-to-all-done.1 = bf16[48,32,512]{2,0,1:T(8,128)(2,1)S(1)} async-done(((bf16[48,32,512]{2,0,1:T(8,128)(2,1)}), bf16[48,32,512]{2,0,1:T(8,128)(2,1)S(1)}, u32[]{:S(2)}, u32[]{:S(2)}) %all-to-all-start.1) | async-done | bytes 1572896 | tf_op jit(solution)/shard_map/all_to_all | solution.py:266
  105.8 1.2 copy-done.4
  107.0 0.9 copy-done.11
  108.0 34.4 %summed0.1.matrix_ref = f32[1536,128]{1,0:T(8,128)S(1)} custom-call(f32[512,128]{1,0:T(8,128)S(1)} %copy-done.11, bf16[512,1024]{1,0:T(8,128)(2,1)S(1)} %copy-done.4, bf16[512,1024]{1,0:T(8,128)(2,1)S(1)} %get-tuple-element.2.refs_1_, bf16[1536,512]{1,0:T(8,128)(2,1)S(1)} %bitcast.43, f32[1536,1]{1,0:T(8,128)S(1)} %bitcast.51), custom_call_target="tpu_custom_call" | custom-call | tf_op jit(solution)/shard_map/summed0/pallas_call | solution.py:182
  142.4 0.0 copy-start.10
  142.4 0.9 copy-done.10
  143.3 7.7 %orth.3 = f32[1536,128]{1,0:T(8,128)} custom-call(f32[1536,128]{1,0:T(8,128)} %copy-done.10), custom_call_target="tpu_custom_call" | custom-call | tf_op jit(solution)/shard_map/orth/pallas_call | solution.py:253
  151.0 1.3 reduce-precision_convert_fusion.3
  152.2 0.0 copy-start.5
  152.2 0.6 convolution_bitcast_fusion.1
  152.8 0.1 reduce-precision_convert_fusion.4
  152.9 0.6 copy-done.5
  153.4 0.5 fusion.18
  153.9 0.0 copy-start.2
  153.9 0.0 copy-start.7
  154.0 0.7 convolution_add_fusion
  154.7 0.1 slice_add_fusion.rows_ref
  154.7 0.8 copy-done.2
  155.5 0.3 copy-done.7
  155.8 36.6 %summed1.1.matrix_ref = f32[2048,128]{1,0:T(8,128)S(1)} custom-call(f32[1024,128]{1,0:T(8,128)S(1)} %slice_add_fusion.rows_ref, bf16[2048,512]{1,0:T(8,128)(2,1)S(1)} %bitcast.48, f32[2048,1]{1,0:T(8,128)S(1)} %bitcast.53), custom_call_target="tpu_custom_call" | custom-call | tf_op jit(solution)/shard_map/summed1/pallas_call | solution.py:182
  192.4 0.0 copy-start.8
  192.4 1.0 copy-done.8
  193.4 8.3 %orth.4 = f32[2048,128]{1,0:T(8,128)} custom-call(f32[2048,128]{1,0:T(8,128)} %copy-done.8), custom_call_target="tpu_custom_call" | custom-call | tf_op jit(solution)/shard_map/orth/pallas_call | solution.py:253
  201.7 1.5 reduce-precision_convert_fusion.1
  203.2 0.4 copy-done.3
  203.6 2.4 fusion.13
  206.0 1.0 convolution_bitcast_fusion
  207.0 0.2 copy-done.6
  207.3 36.1 %summed2.1.matrix_ref = f32[1536,128]{1,0:T(8,128)S(1)} custom-call(f32[512,128]{1,0:T(8,128)S(1)} %slice_add_fusion.1.rows_ref, bf16[512,1024]{1,0:T(8,128)(2,1)S(1)} %copy-done.6, bf16[512,1024]{1,0:T(8,128)(2,1)S(1)} %get-tuple-element.2.refs_1_, bf16[1536,512]{1,0:T(8,128)(2,1)S(1)} %bitcast.45, f32[1536,1]{1,0:T(8,128)S(1)} %bitcast.52), custom_call_target="tpu_custom_call" | custom-call | tf_op jit(solution)/shard_map/summed2/pallas_call | solution.py:182
  243.4 0.0 copy-start.9
  243.4 0.9 copy-done.9
  244.2 8.0 %orth.5 = f32[1536,128]{1,0:T(8,128)} custom-call(f32[1536,128]{1,0:T(8,128)} %copy-done.9), custom_call_target="tpu_custom_call" | custom-call | tf_op jit(solution)/shard_map/orth/pallas_call | solution.py:253
  252.2 2.2 fusion.15
  (13 shorter events, 0.1 us)
Async XLA Ops:
  5.5 57.4 %all-to-all-start = ((bf16[64,32,512]{2,0,1:T(8,128)(2,1)}), bf16[64,32,512]{2,0,1:T(8,128)(2,1)S(1)}, u32[]{:S(2)}, u32[]{:S(2)}) async-start(bf16[64,32,512]{2,0,1:T(8,128)(2,1)} %copy.21), calls=%async_computation | async-start | bytes 4194304 | tf_op jit(solution)/shard_map/all_to_all | solution.py:265
  16.8 50.4 %copy-start.17 = (s32[4]{0:T(128)S(1)}, s32[4]{0:T(128)}, u32[]{:S(2)}) copy-start(s32[4]{0:T(128)} %param.10) | copy-start | bytes 52
  16.8 50.4 %copy-start.16 = (s32[4]{0:T(128)S(1)}, s32[4]{0:T(128)}, u32[]{:S(2)}) copy-start(s32[4]{0:T(128)} %param.11) | copy-start | bytes 52
  16.8 52.2 %copy-start.14 = (s32[4,4]{1,0:T(4,128)S(1)}, s32[4,4]{1,0:T(4,128)}, u32[]{:S(2)}) copy-start(s32[4,4]{1,0:T(4,128)} %param.13) | copy-start | bytes 196
  16.8 52.3 %copy-start.15 = (s32[4,4]{1,0:T(4,128)S(1)}, s32[4,4]{1,0:T(4,128)}, u32[]{:S(2)}) copy-start(s32[4,4]{1,0:T(4,128)} %param.14) | copy-start | bytes 196
  16.8 52.4 %copy-start.13 = (bf16[4,4,128,128]{3,2,1,0:T(8,128)(2,1)S(1)}, bf16[4,4,128,128]{3,2,1,0:T(8,128)(2,1)}, u32[]{:S(2)}) copy-start(bf16[4,4,128,128]{3,2,1,0:T(8,128)(2,1)} %param.12) | copy-start | bytes 1572868
  62.9 1.3 copy-start
  64.2 41.6 %all-to-all-start.1 = ((bf16[48,32,512]{2,0,1:T(8,128)(2,1)}), bf16[48,32,512]{2,0,1:T(8,128)(2,1)S(1)}, u32[]{:S(2)}, u32[]{:S(2)}) async-start(bf16[48,32,512]{2,0,1:T(8,128)(2,1)} %copy.23), calls=%async_computation.1 | async-start | bytes 3145728 | tf_op jit(solution)/shard_map/all_to_all | solution.py:266
  70.1 1.6 copy-start.12
  71.8 1.6 copy-start.1
  105.8 1.2 copy-start.4
  107.0 0.9 copy-start.11
  142.4 0.9 copy-start.10
  152.2 1.2 copy-start.5
  153.9 1.6 copy-start.2
  153.9 1.8 copy-start.7
  192.4 1.0 copy-start.8
  201.7 1.9 copy-start.3
  206.0 1.2 copy-start.6
  243.4 0.9 copy-start.9
